TPU v7x, 512 devices: a whole 4x4x16 slice. The times are simulated.
512 devices in a mesh: tm: 16 (over x, y), tile: 32 (over z, core).
Axes of the slice: x: 4, y: 4, z: 16, core: 2. Of those that a mesh axis runs over, the one named last changes fastest.
Arguments:
- haar_video: bfloat16 [64, 128, 6144], P('tm', 'tile'), may hold values from -6 to 6
- clip_lengths: int32 [16], replicated, may hold values from 1 to 8, 64 in all
- block_owner: int32 [16], replicated, may hold values from 0 to 15, each once
- spatial_in: bfloat16 [3, 3, 48, 128], replicated, may hold values from -0.3125 to 0.3125
- temporal_in: bfloat16 [3, 128, 128], replicated, may hold values from -0.3125 to 0.3125
- bias_in: float32 [128], replicated, may hold values from -4 to 4
- spatial_down: bfloat16 [3, 3, 128, 256], replicated, may hold values from -0.25 to 0.25
- temporal_down: bfloat16 [3, 256, 256], replicated, may hold values from -0.25 to 0.25
- bias_down: float32 [256], replicated, may hold values from -4 to 4
- spatial_out: bfloat16 [3, 3, 256, 256], replicated, may hold values from -0.1875 to 0.1875
- temporal_out: bfloat16 [3, 256, 256], replicated, may hold values from -0.25 to 0.25
- bias_out: float32 [256], replicated, may hold values from -3 to 3
Outputs:
- latents: bfloat16 [32, 64, 64, 256], P('tm', 'tile')
Inputs may be any that keep to these rules, and one draw needn't show every extreme that they name: `clip_lengths`: the clip lengths sum to 64; the longest is exactly 8. `block_owner`: every tm index is named exactly once.
All inputs are finite; a program needn't handle non-finite values.
Results may differ from a plain program's by a relative error of at most 0.015.
Values may be sent and summed in bfloat16 or wider, within the bound.
A program may use at most 64 MiB of HBM per device.

v0:
```python
from functools import partial
import jax
import jax.numpy as jnp
from jax import lax
from jax.sharding import PartitionSpec as P


def padded_2(block, sides, width):
    for axis, dim in sides:
        count = lax.axis_size(axis)
        forward = [(i, i + 1) for i in range(count - 1)]
        backward = [(target, source) for source, target in forward]
        low = lax.ppermute(
            lax.slice_in_dim(block, block.shape[dim] - width, None, axis=dim), axis, forward
        )
        high = lax.ppermute(lax.slice_in_dim(block, 0, width, axis=dim), axis, backward)
        block = jnp.concatenate([low, block, high], axis=dim)
    return block


def passed_along(block, axis, distance):
    devices = range(lax.axis_size(axis))
    route = [(i - distance, i) for i in devices if i - distance in devices]
    return lax.ppermute(block, axis, route)


def clip_of(frame_ids, clip_lengths):
    clip_ends = jnp.cumsum(clip_lengths)
    return jnp.sum((clip_ends[None, :] <= frame_ids[:, None]).astype(jnp.int32), axis=1)


def tap_mask(key_frames, tap_frames, clip_lengths):
    tap_clips = clip_of(tap_frames.reshape(-1), clip_lengths).reshape(tap_frames.shape)
    same_clip = tap_clips == clip_of(key_frames, clip_lengths)[:, None]
    return jnp.where(same_clip & (tap_frames >= 0), 1.0, 0.0).astype(jnp.bfloat16)


def spatial_conv(row_extended, kernel, stride, out_rows, out_cols):
    pad_right = 1 if stride == 1 else 0
    padded = jnp.pad(row_extended, ((0, 0), (0, 0), (1, pad_right), (0, 0)))
    pieces = [
        padded[
            :,
            row_tap : row_tap + stride * out_rows : stride,
            col_tap : col_tap + stride * out_cols : stride,
        ]
        for row_tap in range(3)
        for col_tap in range(3)
    ]
    patches = jnp.concatenate(pieces, axis=-1)
    flattened = jnp.dot(
        patches.reshape(-1, patches.shape[-1]),
        kernel.reshape(-1, kernel.shape[-1]),
        preferred_element_type=jnp.float32,
    )
    return flattened.reshape(patches.shape[:-1] + (kernel.shape[-1],))


def temporal_conv(extended, kernel, mask, out_count, stride, bias, activate):
    running = None
    for lag in range(3):
        tap_frames = extended[lag : lag + stride * out_count : stride] * mask[:, lag].reshape(
            (-1, 1, 1, 1)
        )
        tap_term = jnp.dot(
            tap_frames.reshape(-1, tap_frames.shape[-1]),
            kernel[lag],
            preferred_element_type=jnp.float32,
        )
        running = tap_term if running is None else running + tap_term
    running = running + bias
    if activate:
        running = jax.nn.silu(running)
    return running.reshape(tap_frames.shape[:-1] + (kernel.shape[-1],)).astype(jnp.bfloat16)


def pick_rows(running, shard_piece, first_row, owners, my_index, block_span):
    row_total = shard_piece.shape[0]
    row_ids = jnp.arange(row_total, dtype=jnp.int32)
    block_ids = row_ids // block_span
    slot_ids = jnp.arange(owners.shape[0], dtype=jnp.int32)
    owner_of = jnp.sum(
        jnp.where(block_ids[:, None] == slot_ids[None, :], owners[None, :], 0), axis=1
    )
    position = row_ids % block_span
    span_ids = jnp.arange(block_span, dtype=jnp.int32)
    select = ((position[None, :] == span_ids[:, None]) & (owner_of[None, :] == my_index)).astype(
        jnp.bfloat16
    )
    return jnp.dot(select, shard_piece, preferred_element_type=jnp.float32)


def third_mask(block_index, reduced_count, clip_lengths):
    reduced_ids = block_index * reduced_count + jnp.arange(reduced_count, dtype=jnp.int32)
    lags = jnp.arange(3, dtype=jnp.int32)
    reduced_taps = reduced_ids[:, None] + lags[None, :] - 2
    return tap_mask(2 * reduced_ids + 1, 2 * reduced_taps + 1, clip_lengths)


def per_device(
    haar_video,
    clip_lengths,
    block_owner,
    spatial_in,
    temporal_in,
    bias_in,
    spatial_down,
    temporal_down,
    bias_down,
    spatial_out,
    temporal_out,
    bias_out,
):
    frame_count, row_count, flat_width = haar_video.shape
    in_channels = spatial_in.shape[2]
    col_count = flat_width // in_channels
    frames = haar_video.reshape(frame_count, row_count, col_count, in_channels)
    my_index = lax.axis_index("tm")
    lags = jnp.arange(3, dtype=jnp.int32)
    row_extended = padded_2(frames, (("tile", 1),), 1)
    spatial_one = spatial_conv(row_extended, spatial_in, 1, row_count, col_count).astype(
        jnp.bfloat16
    )
    context = passed_along(spatial_one[frame_count - 2 :], "tm", 1)
    extended = jnp.concatenate([context, spatial_one], axis=0)
    frame_ids = my_index * frame_count + jnp.arange(frame_count, dtype=jnp.int32)
    causal_mask = tap_mask(frame_ids, frame_ids[:, None] + lags[None, :] - 2, clip_lengths)
    hidden_one = temporal_conv(extended, temporal_in, causal_mask, frame_count, 1, bias_in, True)
    upper_row = passed_along(hidden_one[:, row_count - 1 :], "tile", 1)
    row_extended = jnp.concatenate([upper_row, hidden_one], axis=1)
    reduced_rows = row_count // 2
    reduced_cols = col_count // 2
    reduced_count = frame_count // 2
    spatial_two = spatial_conv(row_extended, spatial_down, 2, reduced_rows, reduced_cols).astype(
        jnp.bfloat16
    )
    prior_frame = passed_along(spatial_two[frame_count - 1 :], "tm", 1)
    extended = jnp.concatenate([prior_frame, spatial_two], axis=0)
    reduced_ids = my_index * reduced_count + jnp.arange(reduced_count, dtype=jnp.int32)
    strided_mask = tap_mask(
        2 * reduced_ids + 1, 2 * reduced_ids[:, None] + lags[None, :] - 1, clip_lengths
    )
    hidden_two = temporal_conv(
        extended, temporal_down, strided_mask, reduced_count, 2, bias_down, True
    )
    context = passed_along(hidden_two, "tm", 1)
    extended = jnp.concatenate([context, hidden_two], axis=0)
    block_span = extended.shape[0]
    flattened = extended.reshape(block_span, -1)
    gather_fn = partial(pick_rows, owners=block_owner, my_index=my_index, block_span=block_span)
    moved_block = gather_fn(
        jnp.zeros(flattened.shape, jnp.float32),
        lax.all_gather(flattened, "tm", axis=0, tiled=True),
        jnp.int32(0),
    )
    moved_block = moved_block.astype(jnp.bfloat16).reshape(extended.shape)
    slot_ids = jnp.arange(block_owner.shape[0], dtype=jnp.int32)
    source_block = jnp.sum(jnp.where(block_owner == my_index, slot_ids, 0))
    row_extended = padded_2(moved_block, (("tile", 1),), 1)
    spatial_three = spatial_conv(row_extended, spatial_out, 1, reduced_rows, reduced_cols).astype(
        jnp.bfloat16
    )
    last_mask = third_mask(source_block, reduced_count, clip_lengths)
    final_block = temporal_conv(
        spatial_three, temporal_out, last_mask, reduced_count, 1, bias_out, False
    )
    return final_block


def solution(mesh):
    placed = (P("tm", "tile", None), P(), P(), P(), P(), P(), P(), P(), P(), P(), P(), P())
    return jax.shard_map(
        per_device,
        mesh=mesh,
        in_specs=placed,
        out_specs=P("tm", "tile", None, None),
        check_vma=False,
    )
```

profile of v0, /device:TPU:97, one launch (start us, length us, event | category | flops | bytes accessed | tf_op | source)
XLA Modules:
  0.0 164.6 jit_solution(17710069117527432567)
XLA Ops:
  6.5 1.5 reshape.216
  8.1 0.2 copy.28
  8.3 5.3 %collective-permute-start = (bf16[4,1,128,48]{2,3,1,0:T(8,128)(2,1)S(1)}, bf16[4,1,128,48]{2,3,1,0:T(8,128)(2,1)S(1)}, u32[]{:S(2)}, u32[]{:S(2)}) collective-permute-start(bf16[4,1,128,48]{2,3,1,0:T(8,128)(2,1)S(1)} %get-tuple-element.28), channel_id=1, source_target_pairs={{0,1},{1,2},{2,3},{3,4},{4,5},{5,6},{6,7},{7,8},{8,9},{9,10},{10,1... | collective-permute-start | bytes 147464 | tf_op jit(solution)/shard_map/ppermute | solution.py:13
  13.6 1.9 %collective-permute-start.1 = (bf16[4,1,128,48]{2,3,1,0:T(8,128)(2,1)S(1)}, bf16[4,1,128,48]{2,3,1,0:T(8,128)(2,1)S(1)}, u32[]{:S(2)}, u32[]{:S(2)}) collective-permute-start(bf16[4,1,128,48]{2,3,1,0:T(8,128)(2,1)S(1)} %get-tuple-element.29), channel_id=1, source_target_pairs={{1,0},{2,1},{3,2},{4,3},{5,4},{6,5},{7,6},{8,7},{9,8},{10,9},{11,1... | collective-permute-start | bytes 147464 | tf_op jit(solution)/shard_map/ppermute | solution.py:16
  15.7 0.7 copy.34
  17.1 1.3 fusion.55
  19.4 0.8 collective-permute-done.1
  20.3 0.3 fusion.16
  21.4 0.8 convolution_convert_fusion.1
  22.3 3.2 %collective-permute-start.2 = (bf16[2,4,128,128]{3,2,1,0:T(8,128)(2,1)S(1)}, bf16[2,4,128,128]{3,2,1,0:T(8,128)(2,1)S(1)}, u32[]{:S(2)}, u32[]{:S(2)}) collective-permute-start(bf16[2,4,128,128]{3,2,1,0:T(8,128)(2,1)S(1)} %slice.252), channel_id=1, source_target_pairs={{0,32},{32,64},{64,96},{96,128},{128,160},{160,192},{192,224},{224... | collective-permute-start | bytes 786440 | tf_op jit(solution)/shard_map/ppermute | solution.py:24
  25.5 0.2 convert_reduce_fusion.1
  25.8 0.2 slice_reduce_fusion
  26.0 0.2 fusion.50
  26.2 4.0 %collective-permute-done.2 = bf16[2,4,128,128]{3,2,1,0:T(8,128)(2,1)S(1)} collective-permute-done((bf16[2,4,128,128]{3,2,1,0:T(8,128)(2,1)S(1)}, bf16[2,4,128,128]{3,2,1,0:T(8,128)(2,1)S(1)}, u32[]{:S(2)}, u32[]{:S(2)}) %collective-permute-start.2) | collective-permute-done | bytes 262176 | tf_op jit(solution)/shard_map/ppermute | solution.py:24
  30.5 0.3 fusion.42
  30.7 0.3 convolution_add_fusion.1
  31.1 0.5 multiply_convert_fusion
  31.6 4.4 %collective-permute-start.3 = (bf16[4,1,128,128]{3,2,1,0:T(8,128)(2,1)S(1)}, bf16[4,1,128,128]{3,2,1,0:T(8,128)(2,1)S(1)}, u32[]{:S(2)}, u32[]{:S(2)}) collective-permute-start(bf16[4,1,128,128]{3,2,1,0:T(8,128)(2,1)S(1)} %slice.255), channel_id=1, source_target_pairs={{0,1},{1,2},{2,3},{3,4},{4,5},{5,6},{6,7},{7,8},{8,9},{9,10},{10,1... | collective-permute-start | bytes 393224 | tf_op jit(solution)/shard_map/ppermute | solution.py:24
  36.0 0.2 slice_reduce_fusion.6
  36.2 1.6 collective-permute-done.3
  38.1 0.3 slice.206
  38.4 0.3 slice.207
  38.7 0.3 slice.208
  39.0 0.3 slice.209
  39.4 0.3 slice.210
  39.7 0.3 slice.211
  40.0 0.4 slice.212
  40.5 0.4 slice.213
  40.9 0.8 slice.214
  42.1 0.7 copy-done.6
  42.8 0.5 convolution_convert_fusion.3
  43.4 4.1 %collective-permute-start.4 = (bf16[1,2,64,256]{3,2,1,0:T(8,128)(2,1)S(1)}, bf16[1,2,64,256]{3,2,1,0:T(8,128)(2,1)S(1)}, u32[]{:S(2)}, u32[]{:S(2)}) collective-permute-start(bf16[1,2,64,256]{3,2,1,0:T(8,128)(2,1)S(1)} %slice.256), channel_id=1, source_target_pairs={{0,32},{32,64},{64,96},{96,128},{128,160},{160,192},{192,224},{224... | collective-permute-start | bytes 196616 | tf_op jit(solution)/shard_map/ppermute | solution.py:24
  47.6 1.2 collective-permute-done.4
  49.4 0.2 multiply_convert_fusion.1
  49.6 3.8 %collective-permute-start.5 = (bf16[2,2,64,256]{3,2,1,0:T(8,128)(2,1)S(1)}, bf16[2,2,64,256]{3,2,1,0:T(8,128)(2,1)S(1)}, u32[]{:S(2)}, u32[]{:S(2)}) collective-permute-start(bf16[2,2,64,256]{3,2,1,0:T(8,128)(2,1)S(1)} %bitcast.94), channel_id=1, source_target_pairs={{0,32},{32,64},{64,96},{96,128},{128,160},{160,192},{192,224},{224... | collective-permute-start | bytes 393224 | tf_op jit(solution)/shard_map/ppermute | solution.py:24
  53.4 2.7 %collective-permute-done.5 = bf16[2,2,64,256]{3,2,1,0:T(8,128)(2,1)S(1)} collective-permute-done((bf16[2,2,64,256]{3,2,1,0:T(8,128)(2,1)S(1)}, bf16[2,2,64,256]{3,2,1,0:T(8,128)(2,1)S(1)}, u32[]{:S(2)}, u32[]{:S(2)}) %collective-permute-start.5) | collective-permute-done | bytes 131104 | tf_op jit(solution)/shard_map/ppermute | solution.py:24
  56.2 0.9 reshape.236
  57.2 75.2 %all-gather.3.cloned.1.call-done = bf16[16,4,32768]{2,1,0:T(4,128)(2,1)} async-done(((bf16[1,4,32768]{2,1,0:T(4,128)(2,1)}), bf16[16,4,32768]{2,1,0:T(4,128)(2,1)}) %all-gather.3.cloned.1.call-update) | async-done | bytes 4194320 | tf_op jit(solution)/shard_map/all_gather | solution.py:153
  132.4 7.0 %reshape.237 = bf16[64,32768]{1,0:T(8,128)(2,1)} reshape(bf16[16,4,32768]{2,1,0:T(4,128)(2,1)} %all-gather.3.cloned.1.call-done) | data formatting | bytes 8388608
  139.4 2.8 %convolution_convert_fusion = bf16[4,32768]{1,0:T(4,128)(2,1)S(1)} fusion(bf16[64,32768]{1,0:T(8,128)(2,1)} %reshape.237, s32[64]{0:T(128)S(1)} %and_select_fusion.3, pred[64]{0:T(512)(128)(4,1)S(1)} %broadcast_compare_fusion), kind=kOutput, calls=%fused_computation | convolution fusion | flops 16908800 | bytes 4456768 | tf_op jit(solution)/shard_map/dot_general | solution.py:90
  142.3 5.0 %collective-permute-start.6 = (bf16[4,1,64,256]{3,2,1,0:T(8,128)(2,1)S(1)}, bf16[4,1,64,256]{3,2,1,0:T(8,128)(2,1)S(1)}, u32[]{:S(2)}, u32[]{:S(2)}) collective-permute-start(bf16[4,1,64,256]{3,2,1,0:T(8,128)(2,1)S(1)} %get-tuple-element.24), channel_id=1, source_target_pairs={{0,1},{1,2},{2,3},{3,4},{4,5},{5,6},{6,7},{7,8},{8,9},{9,10},{10,1... | collective-permute-start | bytes 393224 | tf_op jit(solution)/shard_map/ppermute | solution.py:13
  147.3 1.9 %collective-permute-start.7 = (bf16[4,1,64,256]{3,2,1,0:T(8,128)(2,1)S(1)}, bf16[4,1,64,256]{3,2,1,0:T(8,128)(2,1)S(1)}, u32[]{:S(2)}, u32[]{:S(2)}) collective-permute-start(bf16[4,1,64,256]{3,2,1,0:T(8,128)(2,1)S(1)} %get-tuple-element.25), channel_id=1, source_target_pairs={{1,0},{2,1},{3,2},{4,3},{5,4},{6,5},{7,6},{8,7},{9,8},{10,9},{11,1... | collective-permute-start | bytes 393224 | tf_op jit(solution)/shard_map/ppermute | solution.py:16
  149.3 0.2 slice_reduce_fusion.3
  149.5 5.3 %collective-permute-done.7 = bf16[4,1,64,256]{3,2,1,0:T(8,128)(2,1)S(1)} collective-permute-done((bf16[4,1,64,256]{3,2,1,0:T(8,128)(2,1)S(1)}, bf16[4,1,64,256]{3,2,1,0:T(8,128)(2,1)S(1)}, u32[]{:S(2)}, u32[]{:S(2)}) %collective-permute-start.7) | collective-permute-done | bytes 131104 | tf_op jit(solution)/shard_map/ppermute | solution.py:16
  154.8 0.2 fusion.18
  155.4 0.8 convolution_convert_fusion.2
  156.6 0.2 convolution_add_fusion.3
  156.9 0.8 fusion.7
  (89 shorter events, 4.7 us)
Async XLA Ops:
  6.5 148.8 %copy-start = (bf16[3,3,256,256]{3,2,1,0:T(8,128)(2,1)S(1)}, bf16[3,3,256,256]{3,2,1,0:T(8,128)(2,1)}, u32[]{:S(2)}) copy-start(bf16[3,3,256,256]{3,2,1,0:T(8,128)(2,1)} %param.21) | copy-start | bytes 3538948
  6.5 125.9 %all-gather.3.cloned.1.call-start = ((), (), s32[]{:S(2)}) async-start(), calls=%async_computation | async-start | bytes 4456448 | tf_op jit(solution)/shard_map/all_gather | solution.py:153
  8.3 11.1 %collective-permute-start = (bf16[4,1,128,48]{2,3,1,0:T(8,128)(2,1)S(1)}, bf16[4,1,128,48]{2,3,1,0:T(8,128)(2,1)S(1)}, u32[]{:S(2)}, u32[]{:S(2)}) collective-permute-start(bf16[4,1,128,48]{2,3,1,0:T(8,128)(2,1)S(1)} %get-tuple-element.28), channel_id=1, source_target_pairs={{0,1},{1,2},{2,3},{3,4},{4,5},{5,6},{6,7},{7,8},{8,9},{9,10},{10,1... | collective-permute-start | bytes 147464 | tf_op jit(solution)/shard_map/ppermute | solution.py:13
  13.6 6.6 %collective-permute-start.1 = (bf16[4,1,128,48]{2,3,1,0:T(8,128)(2,1)S(1)}, bf16[4,1,128,48]{2,3,1,0:T(8,128)(2,1)S(1)}, u32[]{:S(2)}, u32[]{:S(2)}) collective-permute-start(bf16[4,1,128,48]{2,3,1,0:T(8,128)(2,1)S(1)} %get-tuple-element.29), channel_id=1, source_target_pairs={{1,0},{2,1},{3,2},{4,3},{5,4},{6,5},{7,6},{8,7},{9,8},{10,9},{11,1... | collective-permute-start | bytes 147464 | tf_op jit(solution)/shard_map/ppermute | solution.py:16
  20.5 0.9 copy-start.3
  22.3 8.2 %copy-start.4 = (bf16[3,128,128]{2,1,0:T(8,128)(2,1)S(1)}, bf16[3,128,128]{2,1,0:T(8,128)(2,1)}, u32[]{:S(2)}) copy-start(bf16[3,128,128]{2,1,0:T(8,128)(2,1)} %param.16) | copy-start | bytes 294916
  22.3 8.0 %collective-permute-start.2 = (bf16[2,4,128,128]{3,2,1,0:T(8,128)(2,1)S(1)}, bf16[2,4,128,128]{3,2,1,0:T(8,128)(2,1)S(1)}, u32[]{:S(2)}, u32[]{:S(2)}) collective-permute-start(bf16[2,4,128,128]{3,2,1,0:T(8,128)(2,1)S(1)} %slice.252), channel_id=1, source_target_pairs={{0,32},{32,64},{64,96},{96,128},{128,160},{160,192},{192,224},{224... | collective-permute-start | bytes 786440 | tf_op jit(solution)/shard_map/ppermute | solution.py:24
  30.4 0.7 copy-start.8
  31.6 6.3 %collective-permute-start.3 = (bf16[4,1,128,128]{3,2,1,0:T(8,128)(2,1)S(1)}, bf16[4,1,128,128]{3,2,1,0:T(8,128)(2,1)S(1)}, u32[]{:S(2)}, u32[]{:S(2)}) collective-permute-start(bf16[4,1,128,128]{3,2,1,0:T(8,128)(2,1)S(1)} %slice.255), channel_id=1, source_target_pairs={{0,1},{1,2},{2,3},{3,4},{4,5},{5,6},{6,7},{7,8},{8,9},{9,10},{10,1... | collective-permute-start | bytes 393224 | tf_op jit(solution)/shard_map/ppermute | solution.py:24
  41.8 1.1 copy-start.6
  42.8 6.1 %copy-start.2 = (bf16[3,256,256]{2,1,0:T(8,128)(2,1)S(1)}, bf16[3,256,256]{2,1,0:T(8,128)(2,1)}, u32[]{:S(2)}) copy-start(bf16[3,256,256]{2,1,0:T(8,128)(2,1)} %param.19) | copy-start | bytes 1179652
  43.4 6.0 %copy-start.7 = (f32[256]{0:T(256)S(1)}, f32[256]{0:T(256)}, u32[]{:S(2)}) copy-start(f32[256]{0:T(256)} %param.20) | copy-start | bytes 3076
  43.4 5.4 %collective-permute-start.4 = (bf16[1,2,64,256]{3,2,1,0:T(8,128)(2,1)S(1)}, bf16[1,2,64,256]{3,2,1,0:T(8,128)(2,1)S(1)}, u32[]{:S(2)}, u32[]{:S(2)}) collective-permute-start(bf16[1,2,64,256]{3,2,1,0:T(8,128)(2,1)S(1)} %slice.256), channel_id=1, source_target_pairs={{0,32},{32,64},{64,96},{96,128},{128,160},{160,192},{192,224},{224... | collective-permute-start | bytes 196616 | tf_op jit(solution)/shard_map/ppermute | solution.py:24
  49.1 8.0 %copy-start.9 = (s32[16]{0:T(128)S(1)}, s32[16]{0:T(128)}, u32[]{:S(2)}) copy-start(s32[16]{0:T(128)} %param.14) | copy-start | bytes 196
  49.6 6.5 %collective-permute-start.5 = (bf16[2,2,64,256]{3,2,1,0:T(8,128)(2,1)S(1)}, bf16[2,2,64,256]{3,2,1,0:T(8,128)(2,1)S(1)}, u32[]{:S(2)}, u32[]{:S(2)}) collective-permute-start(bf16[2,2,64,256]{3,2,1,0:T(8,128)(2,1)S(1)} %bitcast.94), channel_id=1, source_target_pairs={{0,32},{32,64},{64,96},{96,128},{128,160},{160,192},{192,224},{224... | collective-permute-start | bytes 393224 | tf_op jit(solution)/shard_map/ppermute | solution.py:24
  142.3 7.2 %collective-permute-start.6 = (bf16[4,1,64,256]{3,2,1,0:T(8,128)(2,1)S(1)}, bf16[4,1,64,256]{3,2,1,0:T(8,128)(2,1)S(1)}, u32[]{:S(2)}, u32[]{:S(2)}) collective-permute-start(bf16[4,1,64,256]{3,2,1,0:T(8,128)(2,1)S(1)} %get-tuple-element.24), channel_id=1, source_target_pairs={{0,1},{1,2},{2,3},{3,4},{4,5},{5,6},{6,7},{7,8},{8,9},{9,10},{10,1... | collective-permute-start | bytes 393224 | tf_op jit(solution)/shard_map/ppermute | solution.py:13
  147.3 7.5 %collective-permute-start.7 = (bf16[4,1,64,256]{3,2,1,0:T(8,128)(2,1)S(1)}, bf16[4,1,64,256]{3,2,1,0:T(8,128)(2,1)S(1)}, u32[]{:S(2)}, u32[]{:S(2)}) collective-permute-start(bf16[4,1,64,256]{3,2,1,0:T(8,128)(2,1)S(1)} %get-tuple-element.25), channel_id=1, source_target_pairs={{1,0},{2,1},{3,2},{4,3},{5,4},{6,5},{7,6},{8,7},{9,8},{10,9},{11,1... | collective-permute-start | bytes 393224 | tf_op jit(solution)/shard_map/ppermute | solution.py:16
  155.4 1.0 copy-start.1
  156.2 0.7 copy-start.5
Sparse Core Ops, SparseCore 0:
  57.2 75.2 all-gather.2
where the time goes:
time: 165 us
  waiting for transfers between devices  90.9 us (55%)
  starting transfers between devices  29.6 us (18%)
  local copies, waits for them, and re-layouts  17.6 us (11%)
  between operations  14.7 us (9%)
  matrix products  7.75 us (5%)
  other arithmetic  4.09 us (2%)
    all_gather x1, waiting for transfers between devices, per_device(): lax.all_gather(flattened, 'tm', axis=0, tiled=True)  75.2 us
    ppermute x4, starting transfers between devices, passed_along(): return lax.ppermute(block, axis, route)  15.5 us
    ppermute x2, starting transfers between devices, padded_2(): lax.ppermute(lax.slice_in_dim(block, block.shape[dim] - width, None, axis...  10.3 us
    unnamed x43, local copies, waits for them, and re-layouts  10 us
    ppermute x4, waiting for transfers between devices, passed_along(): return lax.ppermute(block, axis, route)  9.56 us
    ppermute x2, waiting for transfers between devices, padded_2(): lax.ppermute(lax.slice_in_dim(block, 0, width, axis=dim), axis, backward)  6.08 us
    ppermute x2, starting transfers between devices, padded_2(): lax.ppermute(lax.slice_in_dim(block, 0, width, axis=dim), axis, backward)  3.84 us
    slice x9, local copies, waits for them, and re-layouts, spatial_conv(): padded[:, row_tap:row_tap + stride * out_rows:stride, col_tap:col_tap + s...  3.64 us
  transfers between devices with their start and end apart: 9, of which 7 were waited for; matrix products, arithmetic and copies ran while one was open for 3% of the time, Pallas kernels for 0%

commit v1 on v0

--- a/solution.py
+++ b/solution.py
@@ -3,6 +3,13 @@
 import jax.numpy as jnp
 from jax import lax
 from jax.sharding import PartitionSpec as P
+
+
+def swapped_in(value, name, d):
+    size = lax.axis_size(name)
+    blocks = jnp.stack([value for _ in range(size)])
+    blocks = lax.all_to_all(blocks, name, split_axis=0, concat_axis=0)
+    return jnp.concatenate(blocks, axis=d)
 
 
 def padded_2(block, sides, width):
@@ -149,9 +156,7 @@
     flattened = extended.reshape(block_span, -1)
     gather_fn = partial(pick_rows, owners=block_owner, my_index=my_index, block_span=block_span)
     moved_block = gather_fn(
-        jnp.zeros(flattened.shape, jnp.float32),
-        lax.all_gather(flattened, "tm", axis=0, tiled=True),
-        jnp.int32(0),
+        jnp.zeros(flattened.shape, jnp.float32), swapped_in(flattened, "tm", 0), jnp.int32(0)
     )
     moved_block = moved_block.astype(jnp.bfloat16).reshape(extended.shape)
     slot_ids = jnp.arange(block_owner.shape[0], dtype=jnp.int32)

time: 165 us -> 151 us (0.915)
  the two profiles are of different devices: /device:TPU:97 before, /device:TPU:93 now
where the time goes in v1:
time: 151 us; the launch traced here: 150 us
  waiting for transfers between devices  62.7 us (42%)
  starting transfers between devices  53.7 us (36%)
  local copies, waits for them, and re-layouts  20.5 us (14%)
  matrix products  7.73 us (5%)
  other arithmetic  4.09 us (3%)
    all_to_all x1, waiting for transfers between devices, swapped_in(): blocks = lax.all_to_all(blocks, name, split_axis=0, concat_axis=0)  47.5 us
    ppermute x2, starting transfers between devices, padded_2(): lax.ppermute(lax.slice_in_dim(block, block.shape[dim] - width, None, axis...  25.8 us
    ppermute x4, starting transfers between devices, passed_along(): return lax.ppermute(block, axis, route)  16.6 us
    ppermute x4, waiting for transfers between devices, passed_along(): return lax.ppermute(block, axis, route)  11.1 us
    all_to_all x1, starting transfers between devices, swapped_in(): blocks = lax.all_to_all(blocks, name, split_axis=0, concat_axis=0)  7.46 us
    reshape x1, local copies, waits for them, and re-layouts, swapped_in(): return jnp.concatenate(blocks, axis=d)  6.98 us
    ppermute x2, waiting for transfers between devices, padded_2(): lax.ppermute(lax.slice_in_dim(block, 0, width, axis=dim), axis, backward)  4.05 us
    ppermute x2, starting transfers between devices, padded_2(): lax.ppermute(lax.slice_in_dim(block, 0, width, axis=dim), axis, backward)  3.84 us
  transfers between devices with their start and end apart: 9, of which 6 were waited for; matrix products, arithmetic and copies ran while one was open for 3% of the time, Pallas kernels for 0%

profile of v1, /device:TPU:93, one launch (start us, length us, event | category | flops | bytes accessed | tf_op | source)
XLA Modules:
  0.0 150.0 jit_solution(3786855627471090038)
XLA Ops:
  0.0 1.5 %reshape.218 = bf16[4,4,128,48]{3,2,1,0:T(8,128)(2,1)S(1)} reshape(bf16[4,4,6144]{2,1,0:T(4,128)(2,1)} %param.12) | data formatting | bytes 393216 | tf_op jit(solution)/shard_map/reshape | solution.py:124
  1.6 0.2 copy.21
  1.8 4.1 %collective-permute-start = (bf16[4,1,128,48]{2,3,1,0:T(8,128)(2,1)S(1)}, bf16[4,1,128,48]{2,3,1,0:T(8,128)(2,1)S(1)}, u32[]{:S(2)}, u32[]{:S(2)}) collective-permute-start(bf16[4,1,128,48]{2,3,1,0:T(8,128)(2,1)S(1)} %get-tuple-element.28), channel_id=1, source_target_pairs={{0,1},{1,2},{2,3},{3,4},{4,5},{5,6},{6,7},{7,8},{8,9},{9,10},{10,1... | collective-permute-start | bytes 147464 | tf_op jit(solution)/shard_map/ppermute | solution.py:20
  5.9 1.9 %collective-permute-start.1 = (bf16[4,1,128,48]{2,3,1,0:T(8,128)(2,1)S(1)}, bf16[4,1,128,48]{2,3,1,0:T(8,128)(2,1)S(1)}, u32[]{:S(2)}, u32[]{:S(2)}) collective-permute-start(bf16[4,1,128,48]{2,3,1,0:T(8,128)(2,1)S(1)} %get-tuple-element.29), channel_id=1, source_target_pairs={{1,0},{2,1},{3,2},{4,3},{5,4},{6,5},{7,6},{8,7},{9,8},{10,9},{11,1... | collective-permute-start | bytes 147464 | tf_op jit(solution)/shard_map/ppermute | solution.py:23
  8.0 0.7 copy.27
  9.3 1.3 fusion.55
  11.7 0.3 fusion.16
  12.9 0.8 convolution_convert_fusion.1
  13.7 2.5 %collective-permute-start.2 = (bf16[2,4,128,128]{3,2,1,0:T(8,128)(2,1)S(1)}, bf16[2,4,128,128]{3,2,1,0:T(8,128)(2,1)S(1)}, u32[]{:S(2)}, u32[]{:S(2)}) collective-permute-start(bf16[2,4,128,128]{3,2,1,0:T(8,128)(2,1)S(1)} %slice.252), channel_id=1, source_target_pairs={{0,32},{32,64},{64,96},{96,128},{128,160},{160,192},{192,224},{224... | collective-permute-start | bytes 786440 | tf_op jit(solution)/shard_map/ppermute | solution.py:31
  16.2 0.2 convert_reduce_fusion.1
  16.5 0.2 slice_reduce_fusion
  16.7 0.2 fusion.50
  17.0 6.4 %collective-permute-done.2 = bf16[2,4,128,128]{3,2,1,0:T(8,128)(2,1)S(1)} collective-permute-done((bf16[2,4,128,128]{3,2,1,0:T(8,128)(2,1)S(1)}, bf16[2,4,128,128]{3,2,1,0:T(8,128)(2,1)S(1)}, u32[]{:S(2)}, u32[]{:S(2)}) %collective-permute-start.2) | collective-permute-done | bytes 262176 | tf_op jit(solution)/shard_map/ppermute | solution.py:31
  23.5 0.3 fusion.42
  23.8 0.3 convolution_add_fusion.1
  24.2 0.4 multiply_convert_fusion
  24.6 3.7 %collective-permute-start.3 = (bf16[4,1,128,128]{3,2,1,0:T(8,128)(2,1)S(1)}, bf16[4,1,128,128]{3,2,1,0:T(8,128)(2,1)S(1)}, u32[]{:S(2)}, u32[]{:S(2)}) collective-permute-start(bf16[4,1,128,128]{3,2,1,0:T(8,128)(2,1)S(1)} %slice.255), channel_id=1, source_target_pairs={{0,1},{1,2},{2,3},{3,4},{4,5},{5,6},{6,7},{7,8},{8,9},{9,10},{10,1... | collective-permute-start | bytes 393224 | tf_op jit(solution)/shard_map/ppermute | solution.py:31
  28.4 0.2 slice_reduce_fusion.6
  28.7 1.6 %collective-permute-done.3 = bf16[4,1,128,128]{3,2,1,0:T(8,128)(2,1)S(1)} collective-permute-done((bf16[4,1,128,128]{3,2,1,0:T(8,128)(2,1)S(1)}, bf16[4,1,128,128]{3,2,1,0:T(8,128)(2,1)S(1)}, u32[]{:S(2)}, u32[]{:S(2)}) %collective-permute-start.3) | collective-permute-done | bytes 131104 | tf_op jit(solution)/shard_map/ppermute | solution.py:31
  30.5 0.3 slice.206
  30.8 0.3 slice.207
  31.1 0.3 slice.208
  31.5 0.3 slice.209
  31.8 0.3 slice.210
  32.1 0.3 slice.211
  32.4 0.4 slice.212
  32.9 0.4 slice.213
  33.4 0.8 slice.214
  34.6 0.7 copy-done.6
  35.3 0.5 convolution_convert_fusion.3
  35.8 4.6 %collective-permute-start.4 = (bf16[1,2,64,256]{3,2,1,0:T(8,128)(2,1)S(1)}, bf16[1,2,64,256]{3,2,1,0:T(8,128)(2,1)S(1)}, u32[]{:S(2)}, u32[]{:S(2)}) collective-permute-start(bf16[1,2,64,256]{3,2,1,0:T(8,128)(2,1)S(1)} %slice.256), channel_id=1, source_target_pairs={{0,32},{32,64},{64,96},{96,128},{128,160},{160,192},{192,224},{224... | collective-permute-start | bytes 196616 | tf_op jit(solution)/shard_map/ppermute | solution.py:31
  40.5 1.2 collective-permute-done.4
  42.2 0.2 multiply_convert_fusion.1
  42.5 5.8 %collective-permute-start.5 = (bf16[2,2,64,256]{3,2,1,0:T(8,128)(2,1)S(1)}, bf16[2,2,64,256]{3,2,1,0:T(8,128)(2,1)S(1)}, u32[]{:S(2)}, u32[]{:S(2)}) collective-permute-start(bf16[2,2,64,256]{3,2,1,0:T(8,128)(2,1)S(1)} %bitcast.97), channel_id=1, source_target_pairs={{0,32},{32,64},{64,96},{96,128},{128,160},{160,192},{192,224},{224... | collective-permute-start | bytes 393224 | tf_op jit(solution)/shard_map/ppermute | solution.py:31
  48.3 1.9 %collective-permute-done.5 = bf16[2,2,64,256]{3,2,1,0:T(8,128)(2,1)S(1)} collective-permute-done((bf16[2,2,64,256]{3,2,1,0:T(8,128)(2,1)S(1)}, bf16[2,2,64,256]{3,2,1,0:T(8,128)(2,1)S(1)}, u32[]{:S(2)}, u32[]{:S(2)}) %collective-permute-start.5) | collective-permute-done | bytes 131104 | tf_op jit(solution)/shard_map/ppermute | solution.py:31
  50.2 0.2 copy.31
  50.5 3.6 %stack.3 = bf16[16,4,32768]{2,1,0:T(4,128)(2,1)} broadcast(bf16[4,32768]{1,0:T(4,128)(2,1)S(1)} %bitcast.86), dimensions={1,2} | broadcast | bytes 4456448 | tf_op jit(solution)/shard_map/stack | solution.py:10
  54.0 7.5 %all-to-all-start = ((bf16[16,4,32768]{2,1,0:T(4,128)(2,1)}), bf16[16,4,32768]{2,1,0:T(4,128)(2,1)}, u32[]{:S(2)}, u32[]{:S(2)}) async-start(bf16[16,4,32768]{2,1,0:T(4,128)(2,1)} %stack.3), calls=%async_computation | async-start | bytes 8388608 | tf_op jit(solution)/shard_map/all_to_all | solution.py:11
  61.7 47.5 %all-to-all-done = bf16[16,4,32768]{2,1,0:T(4,128)(2,1)} async-done(((bf16[16,4,32768]{2,1,0:T(4,128)(2,1)}), bf16[16,4,32768]{2,1,0:T(4,128)(2,1)}, u32[]{:S(2)}, u32[]{:S(2)}) %all-to-all-start) | async-done | bytes 4194336 | tf_op jit(solution)/shard_map/all_to_all | solution.py:11
  109.2 7.0 %reshape.231 = bf16[64,32768]{1,0:T(8,128)(2,1)} reshape(bf16[16,4,32768]{2,1,0:T(4,128)(2,1)} %all-to-all-done) | data formatting | bytes 8388608 | tf_op jit(solution)/shard_map/reshape | solution.py:12
  116.2 2.8 %convolution_convert_fusion = bf16[4,32768]{1,0:T(4,128)(2,1)S(1)} fusion(bf16[64,32768]{1,0:T(8,128)(2,1)} %reshape.231, s32[64]{0:T(128)S(1)} %and_select_fusion.3, pred[64]{0:T(512)(128)(4,1)S(1)} %broadcast_compare_fusion), kind=kOutput, calls=%fused_computation | convolution fusion | flops 16908800 | bytes 4456768 | tf_op jit(solution)/shard_map/dot_general | solution.py:97
  119.1 21.6 %collective-permute-start.6 = (bf16[4,1,64,256]{3,2,1,0:T(8,128)(2,1)S(1)}, bf16[4,1,64,256]{3,2,1,0:T(8,128)(2,1)S(1)}, u32[]{:S(2)}, u32[]{:S(2)}) collective-permute-start(bf16[4,1,64,256]{3,2,1,0:T(8,128)(2,1)S(1)} %get-tuple-element.24), channel_id=1, source_target_pairs={{0,1},{1,2},{2,3},{3,4},{4,5},{5,6},{6,7},{7,8},{8,9},{9,10},{10,1... | collective-permute-start | bytes 393224 | tf_op jit(solution)/shard_map/ppermute | solution.py:20
  140.7 1.9 %collective-permute-start.7 = (bf16[4,1,64,256]{3,2,1,0:T(8,128)(2,1)S(1)}, bf16[4,1,64,256]{3,2,1,0:T(8,128)(2,1)S(1)}, u32[]{:S(2)}, u32[]{:S(2)}) collective-permute-start(bf16[4,1,64,256]{3,2,1,0:T(8,128)(2,1)S(1)} %get-tuple-element.25), channel_id=1, source_target_pairs={{1,0},{2,1},{3,2},{4,3},{5,4},{6,5},{7,6},{8,7},{9,8},{10,9},{11,1... | collective-permute-start | bytes 393224 | tf_op jit(solution)/shard_map/ppermute | solution.py:23
  142.7 0.2 slice_reduce_fusion.3
  143.0 4.1 %collective-permute-done.7 = bf16[4,1,64,256]{3,2,1,0:T(8,128)(2,1)S(1)} collective-permute-done((bf16[4,1,64,256]{3,2,1,0:T(8,128)(2,1)S(1)}, bf16[4,1,64,256]{3,2,1,0:T(8,128)(2,1)S(1)}, u32[]{:S(2)}, u32[]{:S(2)}) %collective-permute-start.7) | collective-permute-done | bytes 131104 | tf_op jit(solution)/shard_map/ppermute | solution.py:23
  147.0 0.2 fusion.18
  147.6 0.8 convolution_convert_fusion.2
  149.1 0.8 fusion.7
  (89 shorter events, 4.9 us)
Async XLA Ops:
  0.0 147.6 %copy-start = (bf16[3,3,256,256]{3,2,1,0:T(8,128)(2,1)S(1)}, bf16[3,3,256,256]{3,2,1,0:T(8,128)(2,1)}, u32[]{:S(2)}) copy-start(bf16[3,3,256,256]{3,2,1,0:T(8,128)(2,1)} %param.21) | copy-start | bytes 3538948
  1.8 9.9 %collective-permute-start = (bf16[4,1,128,48]{2,3,1,0:T(8,128)(2,1)S(1)}, bf16[4,1,128,48]{2,3,1,0:T(8,128)(2,1)S(1)}, u32[]{:S(2)}, u32[]{:S(2)}) collective-permute-start(bf16[4,1,128,48]{2,3,1,0:T(8,128)(2,1)S(1)} %get-tuple-element.28), channel_id=1, source_target_pairs={{0,1},{1,2},{2,3},{3,4},{4,5},{5,6},{6,7},{7,8},{8,9},{9,10},{10,1... | collective-permute-start | bytes 147464 | tf_op jit(solution)/shard_map/ppermute | solution.py:20
  5.9 5.8 %collective-permute-start.1 = (bf16[4,1,128,48]{2,3,1,0:T(8,128)(2,1)S(1)}, bf16[4,1,128,48]{2,3,1,0:T(8,128)(2,1)S(1)}, u32[]{:S(2)}, u32[]{:S(2)}) collective-permute-start(bf16[4,1,128,48]{2,3,1,0:T(8,128)(2,1)S(1)} %get-tuple-element.29), channel_id=1, source_target_pairs={{1,0},{2,1},{3,2},{4,3},{5,4},{6,5},{7,6},{8,7},{9,8},{10,9},{11,1... | collective-permute-start | bytes 147464 | tf_op jit(solution)/shard_map/ppermute | solution.py:23
  12.0 0.9 copy-start.3
  13.7 9.8 %copy-start.4 = (bf16[3,128,128]{2,1,0:T(8,128)(2,1)S(1)}, bf16[3,128,128]{2,1,0:T(8,128)(2,1)}, u32[]{:S(2)}) copy-start(bf16[3,128,128]{2,1,0:T(8,128)(2,1)} %param.16) | copy-start | bytes 294916
  13.7 9.6 %collective-permute-start.2 = (bf16[2,4,128,128]{3,2,1,0:T(8,128)(2,1)S(1)}, bf16[2,4,128,128]{3,2,1,0:T(8,128)(2,1)S(1)}, u32[]{:S(2)}, u32[]{:S(2)}) collective-permute-start(bf16[2,4,128,128]{3,2,1,0:T(8,128)(2,1)S(1)} %slice.252), channel_id=1, source_target_pairs={{0,32},{32,64},{64,96},{96,128},{128,160},{160,192},{192,224},{224... | collective-permute-start | bytes 786440 | tf_op jit(solution)/shard_map/ppermute | solution.py:31
  23.5 0.7 copy-start.8
  24.6 5.7 %collective-permute-start.3 = (bf16[4,1,128,128]{3,2,1,0:T(8,128)(2,1)S(1)}, bf16[4,1,128,128]{3,2,1,0:T(8,128)(2,1)S(1)}, u32[]{:S(2)}, u32[]{:S(2)}) collective-permute-start(bf16[4,1,128,128]{3,2,1,0:T(8,128)(2,1)S(1)} %slice.255), channel_id=1, source_target_pairs={{0,1},{1,2},{2,3},{3,4},{4,5},{5,6},{6,7},{7,8},{8,9},{9,10},{10,1... | collective-permute-start | bytes 393224 | tf_op jit(solution)/shard_map/ppermute | solution.py:31
  34.2 1.1 copy-start.6
  35.3 6.6 %copy-start.2 = (bf16[3,256,256]{2,1,0:T(8,128)(2,1)S(1)}, bf16[3,256,256]{2,1,0:T(8,128)(2,1)}, u32[]{:S(2)}) copy-start(bf16[3,256,256]{2,1,0:T(8,128)(2,1)} %param.19) | copy-start | bytes 1179652
  35.8 6.4 %copy-start.7 = (f32[256]{0:T(256)S(1)}, f32[256]{0:T(256)}, u32[]{:S(2)}) copy-start(f32[256]{0:T(256)} %param.20) | copy-start | bytes 3076
  35.8 5.9 %collective-permute-start.4 = (bf16[1,2,64,256]{3,2,1,0:T(8,128)(2,1)S(1)}, bf16[1,2,64,256]{3,2,1,0:T(8,128)(2,1)S(1)}, u32[]{:S(2)}, u32[]{:S(2)}) collective-permute-start(bf16[1,2,64,256]{3,2,1,0:T(8,128)(2,1)S(1)} %slice.256), channel_id=1, source_target_pairs={{0,32},{32,64},{64,96},{96,128},{128,160},{160,192},{192,224},{224... | collective-permute-start | bytes 196616 | tf_op jit(solution)/shard_map/ppermute | solution.py:31
  42.5 7.7 %collective-permute-start.5 = (bf16[2,2,64,256]{3,2,1,0:T(8,128)(2,1)S(1)}, bf16[2,2,64,256]{3,2,1,0:T(8,128)(2,1)S(1)}, u32[]{:S(2)}, u32[]{:S(2)}) collective-permute-start(bf16[2,2,64,256]{3,2,1,0:T(8,128)(2,1)S(1)} %bitcast.97), channel_id=1, source_target_pairs={{0,32},{32,64},{64,96},{96,128},{128,160},{160,192},{192,224},{224... | collective-permute-start | bytes 393224 | tf_op jit(solution)/shard_map/ppermute | solution.py:31
  54.0 7.6 %copy-start.9 = (s32[16]{0:T(128)S(1)}, s32[16]{0:T(128)}, u32[]{:S(2)}) copy-start(s32[16]{0:T(128)} %param.14) | copy-start | bytes 196
  54.0 55.2 %all-to-all-start = ((bf16[16,4,32768]{2,1,0:T(4,128)(2,1)}), bf16[16,4,32768]{2,1,0:T(4,128)(2,1)}, u32[]{:S(2)}, u32[]{:S(2)}) async-start(bf16[16,4,32768]{2,1,0:T(4,128)(2,1)} %stack.3), calls=%async_computation | async-start | bytes 8388608 | tf_op jit(solution)/shard_map/all_to_all | solution.py:11
  119.1 23.9 %collective-permute-start.6 = (bf16[4,1,64,256]{3,2,1,0:T(8,128)(2,1)S(1)}, bf16[4,1,64,256]{3,2,1,0:T(8,128)(2,1)S(1)}, u32[]{:S(2)}, u32[]{:S(2)}) collective-permute-start(bf16[4,1,64,256]{3,2,1,0:T(8,128)(2,1)S(1)} %get-tuple-element.24), channel_id=1, source_target_pairs={{0,1},{1,2},{2,3},{3,4},{4,5},{5,6},{6,7},{7,8},{8,9},{9,10},{10,1... | collective-permute-start | bytes 393224 | tf_op jit(solution)/shard_map/ppermute | solution.py:20
  140.7 6.3 %collective-permute-start.7 = (bf16[4,1,64,256]{3,2,1,0:T(8,128)(2,1)S(1)}, bf16[4,1,64,256]{3,2,1,0:T(8,128)(2,1)S(1)}, u32[]{:S(2)}, u32[]{:S(2)}) collective-permute-start(bf16[4,1,64,256]{3,2,1,0:T(8,128)(2,1)S(1)} %get-tuple-element.25), channel_id=1, source_target_pairs={{1,0},{2,1},{3,2},{4,3},{5,4},{6,5},{7,6},{8,7},{9,8},{10,9},{11,1... | collective-permute-start | bytes 393224 | tf_op jit(solution)/shard_map/ppermute | solution.py:23
  147.6 1.0 copy-start.1
  148.4 0.7 copy-start.5
